TPU v7x, 512 devices: a whole 4x4x16 slice. The times are simulated.
512 devices in a mesh: section: 8 (over y, x_lo), tile: 64 (over z, x_hi, core).
Axes of the slice: x: 4 (x_hi: 2, x_lo: 2; x = x_hi * 2 + x_lo), y: 4, z: 16, core: 2. Of those that a mesh axis runs over, the one named last changes fastest.
Arguments:
- block_inputs: bfloat16 [8, 24576, 1536], P('section', 'tile'), may hold values from -6 to 6
- stale_kv: bfloat16 [8, 24576, 3072], P('section', 'tile'), may hold values from -6 to 6
- projection: bfloat16 [8, 3, 1536, 1536], P('section', None, None, 'tile'), may hold values from -0.15625 to 0.15625
- modulation: float32 [8, 3, 1536], P('section'), may hold values from -3 to 3
- pattern: int32 [128, 4], P('tile'), may hold values from 0 to 1, as said below
- order: int32 [2], replicated, may hold values from 0 to 1, each once
Outputs:
- block_outputs: bfloat16 [8, 24576, 1536], P('section', 'tile')
Inputs may be any that keep to these rules, and one draw needn't show every extreme that they name: `pattern`: row i has a 1 at entry 1 + (i mod 2), its own tile, and at entries 0 and 3. `order`: each of the 2 patch groups appears once.
All inputs are finite; a program needn't handle non-finite values.
Results may differ from a plain program's by a relative error of at most 0.0039.
Values may be sent and summed in bfloat16 or wider, within the bound.
A program may use at most 128 MiB of HBM per device.

v0:
```python
import math

import jax
import jax.numpy as jnp
import numpy as np
from jax import lax
from jax.sharding import PartitionSpec as P

HEADS = 12


epsilon = 1e-06


def with_halo(x, sides, width):
    for axis, dim in sides:
        peers, length = (lax.axis_size(axis), x.shape[dim])
        up = [(i, (i + 1) % peers) for i in range(peers - 1)]
        down = [(j, i) for i, j in up]
        last = lax.slice_in_dim(x, length - width, length, axis=dim)
        first = lax.slice_in_dim(x, 0, width, axis=dim)
        before = lax.ppermute(last, axis, up)
        after = lax.ppermute(first, axis, down)
        x = jnp.concatenate([before, x, after], axis=dim)
    return x


def from_behind(value, axis, steps):
    count = lax.axis_size(axis)
    first, last = (max(0, -steps), min(count, count - steps))
    return lax.ppermute(value, axis, [(source, source + steps) for source in range(first, last)])


def modulate(stream, modulation_row):
    values = stream.astype(jnp.float32)
    normed = values * lax.rsqrt(jnp.mean(values * values, axis=-1, keepdims=True) + epsilon)
    return ((1.0 + modulation_row[1]) * normed + modulation_row[0]).astype(jnp.bfloat16)


def head_norm(values, head_count):
    shaped = values.reshape(values.shape[0], head_count, -1)
    shaped = shaped * lax.rsqrt(jnp.mean(shaped * shaped, axis=-1, keepdims=True) + epsilon)
    return shaped.reshape(values.shape).astype(jnp.bfloat16)


def keys_values(hidden, key_weight, value_weight, head_count):
    key_rows = jnp.dot(hidden, key_weight, preferred_element_type=jnp.float32)
    value_rows = jnp.dot(hidden, value_weight, preferred_element_type=jnp.float32)
    return jnp.concatenate(
        [head_norm(key_rows, head_count), value_rows.astype(jnp.bfloat16)], axis=-1
    )


def attend(queries, window, allowed, head_count):
    row_count, feat_width = queries.shape
    head_width = feat_width // head_count
    query_heads = queries.reshape(row_count, head_count, head_width)
    key_heads = window[:, :feat_width].reshape(-1, head_count, head_width)
    value_heads = window[:, feat_width:].reshape(-1, head_count, head_width)
    scores = jnp.einsum(
        "qhd,khd->hqk", query_heads, key_heads, preferred_element_type=jnp.float32
    ) * (1.0 / math.sqrt(head_width))
    unnormed = jnp.exp(scores) * allowed[None].astype(jnp.float32)
    weights_low = (unnormed / jnp.sum(unnormed, axis=-1, keepdims=True)).astype(jnp.bfloat16)
    attended = jnp.einsum(
        "hqk,khd->qhd", weights_low, value_heads, preferred_element_type=jnp.float32
    )
    return attended.reshape(row_count, feat_width)


def shards(block_inputs, stale_kv, projection, modulation, pattern, order):
    tile_count = lax.axis_size("tile")
    section_index = lax.axis_index("section")
    tile_index = lax.axis_index("tile")
    inputs_local = block_inputs[0]
    tok_rows, feat_width = inputs_local.shape
    group_count = order.shape[0]
    tiles_here = pattern.shape[0]
    per_group = tiles_here // group_count
    tile_rows = tok_rows // tiles_here
    rim_rows = tile_rows // 4
    slot_count = tiles_here + 2
    group_rows = per_group * tile_rows
    window_len = tok_rows + 2 * rim_rows
    slot_tokens = np.array([rim_rows] + [tile_rows] * tiles_here + [rim_rows], dtype=np.int32)
    modulation_row = modulation[0]
    stale_local = stale_kv[0]
    gathered = lax.all_gather(projection[0], "tile", axis=2, tiled=True)
    query_weight = gathered[0]
    key_weight = gathered[1]
    value_weight = gathered[2]
    stale_edges = jnp.concatenate(
        [stale_local[:rim_rows], stale_local[tok_rows - rim_rows :]], axis=0
    )
    stale_ext = with_halo(stale_edges, (("tile", 0),), rim_rows)
    lower_start = stale_ext[:rim_rows]
    upper_start = stale_ext[stale_ext.shape[0] - rim_rows :]
    group_ids = jnp.arange(group_count, dtype=jnp.int32)
    slot_ids = jnp.arange(slot_count, dtype=jnp.int32)
    slot_valid = ((slot_ids > 0) | (tile_index > 0)) & (
        (slot_ids < slot_count - 1) | (tile_index < tile_count - 1)
    )
    pattern_groups = (pattern > 0).reshape(per_group, group_count, slot_count)

    def take_group(array, group_id):
        shaped = array.reshape(per_group, group_count, tile_rows, -1)
        picked = lax.dynamic_index_in_dim(shaped, group_id, 1, keepdims=False)
        return picked.reshape(group_rows, -1)

    def put_group(array, new_rows, group_id):
        shaped = array.reshape(per_group, group_count, tile_rows, -1)
        update = new_rows.reshape(per_group, 1, tile_rows, -1)
        return lax.dynamic_update_slice_in_dim(shaped, update, group_id, 1).reshape(array.shape)

    empty_out = jnp.zeros((tok_rows, feat_width), jnp.bfloat16)
    empty_sent = jnp.zeros((group_rows, feat_width), jnp.bfloat16)

    def step_body(step_index, state_tuple):
        held, lower_rim, upper_rim, outputs, outgoing = state_tuple
        incoming = from_behind(outgoing, "section", 1)
        place = jnp.remainder(step_index - section_index, group_count)
        group_id = jnp.sum(jnp.where(group_ids == place, order, 0))
        from_inputs = (section_index == 0) | (step_index == 0)
        stream_in = jnp.where(from_inputs, take_group(inputs_local, group_id), incoming)
        hidden = modulate(stream_in, modulation_row)
        queries = head_norm(
            jnp.dot(hidden, query_weight, preferred_element_type=jnp.float32), HEADS
        )
        fresh_kv = keys_values(hidden, key_weight, value_weight, HEADS)
        kv_buffer = put_group(held, fresh_kv, group_id)
        fresh_edges = jnp.concatenate(
            [fresh_kv[:rim_rows], fresh_kv[group_rows - rim_rows :]], axis=0
        )
        fresh_ext = with_halo(fresh_edges, (("tile", 0),), rim_rows)
        new_lower = jnp.where(
            group_id == (tiles_here - 1) % group_count, fresh_ext[:rim_rows], lower_rim
        )
        new_upper = jnp.where(group_id == 0, fresh_ext[fresh_ext.shape[0] - rim_rows :], upper_rim)
        window = jnp.concatenate([lower_rim, kv_buffer, upper_rim], axis=0)
        tile_allowed = (
            lax.dynamic_index_in_dim(pattern_groups, group_id, 1, keepdims=False)
            & slot_valid[None, :]
        )
        allowed = jnp.repeat(tile_allowed, tile_rows, axis=0)
        allowed = jnp.repeat(allowed, slot_tokens, axis=1, total_repeat_length=window_len)
        attended = attend(queries, window, allowed, HEADS)
        result = (stream_in.astype(jnp.float32) + modulation_row[2] * attended).astype(jnp.bfloat16)
        outputs = put_group(outputs, result, group_id)
        return (kv_buffer, new_lower, new_upper, outputs, result)

    finished = lax.fori_loop(
        0, group_count, step_body, (stale_local, lower_start, upper_start, empty_out, empty_sent)
    )
    return finished[3][None]


def solution(mesh):
    placed = (
        P("section", "tile", None),
        P("section", "tile", None),
        P("section", None, None, "tile"),
        P("section", None, None),
        P("tile", None),
        P(),
    )
    return jax.shard_map(
        shards, mesh=mesh, in_specs=placed, out_specs=P("section", "tile", None), check_vma=False
    )
```

profile of v0, /device:TPU:1, one launch (start us, length us, event | category | flops | bytes accessed | tf_op | source)
XLA Modules:
  0.0 357.9 jit_solution(11009158979189493739)
XLA Ops:
  6.5 3.4 copy.129
  11.0 8.8 %collective-permute-start.4 = (bf16[48,3072]{1,0:T(8,128)(2,1)S(1)}, bf16[48,3072]{1,0:T(8,128)(2,1)}, u32[]{:S(2)}, u32[]{:S(2)}) collective-permute-start(bf16[48,3072]{1,0:T(8,128)(2,1)S(1)} %get-tuple-element.890), channel_id=1, source_target_pairs={{1,0},{2,1},{3,2},{4,3},{5,4},{6,5},{7,6},{8,7},{9,8},{10,9},{11,1... | collective-permute-start | bytes 884744 | tf_op jit(solution)/shard_map/ppermute | solution.py:23
  19.8 1.9 collective-permute-start.3
  21.8 179.9 %all-gather.3.cloned.1.call-done = bf16[1,3,1536,1536]{2,3,1,0:T(8,128)(2,1)} async-done(((bf16[1,3,1536,24]{2,3,1,0:T(8,128)(2,1)}), bf16[1,3,1536,1536]{2,3,1,0:T(8,128)(2,1)}) %all-gather.3.cloned.1.call-update) | async-done | bytes 14155792 | tf_op jit(solution)/shard_map/all_gather | solution.py:88
  201.7 10.8 %slice_bitcast_fusion = (bf16[1536,1536]{0,1:T(8,128)(2,1)}, bf16[1536,1536]{0,1:T(8,128)(2,1)}, bf16[1536,1536]{0,1:T(8,128)(2,1)}) fusion(bf16[1,3,1536,1536]{2,3,1,0:T(8,128)(2,1)} %all-gather.3.cloned.1.call-done), kind=kLoop, calls=%fused_computation.57 | loop fusion | bytes 28311552 | tf_op jit(solution)/shard_map/squeeze | solution.py:89
  212.5 6.6 %copy.64 = bf16[1536,1536]{1,0:T(8,128)(2,1)} copy(bf16[1536,1536]{0,1:T(8,128)(2,1)} %get-tuple-element.887) | data formatting | bytes 9437184
  219.1 6.7 %copy.63 = bf16[1536,1536]{1,0:T(8,128)(2,1)} copy(bf16[1536,1536]{0,1:T(8,128)(2,1)} %get-tuple-element.888) | data formatting | bytes 9437184
  225.8 6.7 %copy.62 = bf16[1536,1536]{1,0:T(8,128)(2,1)} copy(bf16[1536,1536]{0,1:T(8,128)(2,1)} %get-tuple-element.889) | data formatting | bytes 9437184
  232.5 1.1 broadcast_in_dim.76
  233.6 117.5 %while.29 = (s32[]{:T(128)}, bf16[384,3072]{1,0:T(8,128)(2,1)}, bf16[48,3072]{1,0:T(8,128)(2,1)}, bf16[48,3072]{1,0:T(8,128)(2,1)}, bf16[384,1536]{1,0:T(8,128)(...) while((s32[]{:T(128)}, bf16[384,3072]{1,0:T(8,128)(2,1)}, ...), condition=%wide.region_10.11_spmd.clone.clone.clone, body=%wide.region_1.10_spmd.clone.clone.clone.sunk | while | flops 3314392064 | bytes 128456560 | solution.py:151
  233.6 2.2 collective-permute-start
  239.9 1.9 gather_fusion
  242.8 5.5 %collective-permute-done = bf16[192,1536]{1,0:T(8,128)(2,1)S(1)} collective-permute-done((bf16[192,1536]{1,0:T(8,128)(2,1)S(1)}, bf16[192,1536]{1,0:T(8,128)(2,1)S(1)}, u32[]{:S(2)}, u32[]{:S(2)}) %collective-permute-start) | collective-permute-done | bytes 589856 | tf_op jit(solution)/shard_map/while/body/eval_jaxpr/ppermute | solution.py:31
  248.3 1.4 fusion.67
  249.7 4.4 %convolution_convert_fusion.2 = bf16[192,1536]{1,0:T(8,128)(2,1)} fusion(bf16[1536,1536]{1,0:T(8,128)(2,1)} %get-tuple-element.1085, bf16[192,1536]{1,0:T(8,128)(2,1)S(1)} %get-tuple-element.1012, f32[1536]{0:T(1024)S(1)} %get-tuple-element.1013, f32[192]{0:T(256)S(1)} %add_rsqrt_fusion.6, f32[1536]{0:T(1024)S(1)} %get-tuple-element.1015), kind=kOutput, calls=%fused_computation.9.clone.1 | convolution fusion | flops 907739136 | bytes 5911296 | tf_op jit(solution)/shard_map/while/body/eval_jaxpr/dot_general | solution.py:48
  254.1 2.2 fusion.73
  256.3 1.4 mul.474
  258.4 4.9 %fusion.68 = (f32[192,1536]{1,0:T(8,128)}, f32[192,1536]{1,0:T(8,128)}) fusion(bf16[1536,1536]{1,0:T(8,128)(2,1)} %get-tuple-element.1084, bf16[192,1536]{1,0:T(8,128)(2,1)S(1)} %get-tuple-element.1012, f32[1536]{0:T(1024)S(1)} %get-tuple-element.1013, f32[192]{0:T(256)S(1)} %add_rsqrt_fusion.6, f32[1536]{0:T(1024)S(1)} %get-tuple-element.1015), kind=kOutput, calls=%fused_computation.65.clone.1 | convolution fusion | flops 907739136 | bytes 7680768 | tf_op jit(solution)/shard_map/while/body/eval_jaxpr/dot_general | solution.py:47
  263.3 1.4 mul.472
  268.5 4.6 %collective-permute-start.1 = (bf16[48,3072]{1,0:T(8,128)(2,1)}, bf16[48,3072]{1,0:T(8,128)(2,1)}, u32[]{:S(2)}, u32[]{:S(2)}) collective-permute-start(bf16[48,3072]{1,0:T(8,128)(2,1)} %get-tuple-element.1018), channel_id=1, source_target_pairs={{0,1},{1,2},{2,3},{3,4},{4,5},{5,6},{6,7},{7,8},{8,9},{9,10},{10,1... | collective-permute-start | bytes 884744 | tf_op jit(solution)/shard_map/while/body/eval_jaxpr/ppermute | solution.py:22
  273.1 1.9 collective-permute-start.2
  275.1 1.2 fusion.70
  276.3 2.0 pad_maximum_fusion.3
  278.3 1.3 fusion.72
  279.6 1.6 copy.103
  281.2 1.7 copy.105
  283.9 1.6 fusion.74
  286.9 2.0 broadcast_select_fusion.8
  288.9 1.7 broadcast_select_fusion.7
  290.7 3.5 collective-permute-start
  298.2 1.9 gather_fusion
  301.2 5.1 %collective-permute-done = bf16[192,1536]{1,0:T(8,128)(2,1)S(1)} collective-permute-done((bf16[192,1536]{1,0:T(8,128)(2,1)S(1)}, bf16[192,1536]{1,0:T(8,128)(2,1)S(1)}, u32[]{:S(2)}, u32[]{:S(2)}) %collective-permute-start) | collective-permute-done | bytes 589856 | tf_op jit(solution)/shard_map/while/body/eval_jaxpr/ppermute | solution.py:31
  306.2 1.4 fusion.67
  307.6 4.4 %convolution_convert_fusion.2 = bf16[192,1536]{1,0:T(8,128)(2,1)} fusion(bf16[1536,1536]{1,0:T(8,128)(2,1)} %get-tuple-element.1085, bf16[192,1536]{1,0:T(8,128)(2,1)S(1)} %get-tuple-element.1012, f32[1536]{0:T(1024)S(1)} %get-tuple-element.1013, f32[192]{0:T(256)S(1)} %add_rsqrt_fusion.6, f32[1536]{0:T(1024)S(1)} %get-tuple-element.1015), kind=kOutput, calls=%fused_computation.9.clone.1 | convolution fusion | flops 907739136 | bytes 5911296 | tf_op jit(solution)/shard_map/while/body/eval_jaxpr/dot_general | solution.py:48
  312.1 2.2 fusion.73
  314.2 1.4 mul.474
  316.4 4.9 %fusion.68 = (f32[192,1536]{1,0:T(8,128)}, f32[192,1536]{1,0:T(8,128)}) fusion(bf16[1536,1536]{1,0:T(8,128)(2,1)} %get-tuple-element.1084, bf16[192,1536]{1,0:T(8,128)(2,1)S(1)} %get-tuple-element.1012, f32[1536]{0:T(1024)S(1)} %get-tuple-element.1013, f32[192]{0:T(256)S(1)} %add_rsqrt_fusion.6, f32[1536]{0:T(1024)S(1)} %get-tuple-element.1015), kind=kOutput, calls=%fused_computation.65.clone.1 | convolution fusion | flops 907739136 | bytes 7680768 | tf_op jit(solution)/shard_map/while/body/eval_jaxpr/dot_general | solution.py:47
  321.3 1.4 mul.472
  326.4 7.1 %collective-permute-start.1 = (bf16[48,3072]{1,0:T(8,128)(2,1)}, bf16[48,3072]{1,0:T(8,128)(2,1)}, u32[]{:S(2)}, u32[]{:S(2)}) collective-permute-start(bf16[48,3072]{1,0:T(8,128)(2,1)} %get-tuple-element.1018), channel_id=1, source_target_pairs={{0,1},{1,2},{2,3},{3,4},{4,5},{5,6},{6,7},{7,8},{8,9},{9,10},{10,1... | collective-permute-start | bytes 884744 | tf_op jit(solution)/shard_map/while/body/eval_jaxpr/ppermute | solution.py:22
  333.6 1.9 collective-permute-start.2
  335.5 1.2 fusion.70
  336.7 2.0 pad_maximum_fusion.3
  338.6 1.3 fusion.72
  340.0 1.6 copy.103
  341.6 1.7 copy.105
  344.3 1.6 fusion.74
  347.3 2.0 broadcast_select_fusion.8
  349.3 1.7 broadcast_select_fusion.7
  (106 shorter events, 18.5 us)
Async XLA Ops:
  6.5 15.3 %copy-start.10 = (f32[1,3,1536]{2,0,1:T(1,128)S(1)}, f32[1,3,1536]{2,0,1:T(1,128)}, u32[]{:S(2)}) copy-start(f32[1,3,1536]{2,0,1:T(1,128)} %param.14) | copy-start | bytes 55300
  6.5 15.3 %copy-start.11 = (s32[2,4]{1,0:T(2,128)S(1)}, s32[2,4]{1,0:T(2,128)}, u32[]{:S(2)}) copy-start(s32[2,4]{1,0:T(2,128)} %param.15) | copy-start | bytes 100
  6.5 195.2 %all-gather.3.cloned.1.call-start = ((), (), s32[]{:S(2)}) async-start(), calls=%async_computation | async-start | bytes 14376960 | tf_op jit(solution)/shard_map/all_gather | solution.py:88
  11.0 221.4 %collective-permute-start.4 = (bf16[48,3072]{1,0:T(8,128)(2,1)S(1)}, bf16[48,3072]{1,0:T(8,128)(2,1)}, u32[]{:S(2)}, u32[]{:S(2)}) collective-permute-start(bf16[48,3072]{1,0:T(8,128)(2,1)S(1)} %get-tuple-element.890), channel_id=1, source_target_pairs={{1,0},{2,1},{3,2},{4,3},{5,4},{6,5},{7,6},{8,7},{9,8},{10,9},{11,1... | collective-permute-start | bytes 884744 | tf_op jit(solution)/shard_map/ppermute | solution.py:23
  19.8 212.7 %collective-permute-start.3 = (bf16[48,3072]{1,0:T(8,128)(2,1)S(1)}, bf16[48,3072]{1,0:T(8,128)(2,1)}, u32[]{:S(2)}, u32[]{:S(2)}) collective-permute-start(bf16[48,3072]{1,0:T(8,128)(2,1)S(1)} %get-tuple-element.891), channel_id=1, source_target_pairs={{0,1},{1,2},{2,3},{3,4},{4,5},{5,6},{6,7},{7,8},{8,9},{9,10},{10,1... | collective-permute-start | bytes 884744 | tf_op jit(solution)/shard_map/ppermute | solution.py:22
  225.8 7.8 %copy-start.9 = (s32[480]{0:T(512)S(1)}, s32[480]{0:T(512)}, u32[]{:S(2)}) copy-start(s32[480]{0:T(512)} %constant.365) | copy-start | bytes 5764
  225.8 7.8 %copy-start.12 = (s32[2]{0:T(128)S(1)}, s32[2]{0:T(128)}, u32[]{:S(2)}) copy-start(s32[2]{0:T(128)} %param.16) | copy-start | bytes 28
  233.6 9.2 %copy-start.7 = (f32[3,1536]{1,0:T(4,128)}, f32[3,1536]{1,0:T(4,128)S(1)}, u32[]{:S(2)}) copy-start(f32[3,1536]{1,0:T(4,128)S(1)} %get-tuple-element.1079) | copy-start | bytes 55300 | tf_op jit(solution)/shard_map/while
  233.6 14.7 %collective-permute-start = (bf16[192,1536]{1,0:T(8,128)(2,1)S(1)}, bf16[192,1536]{1,0:T(8,128)(2,1)S(1)}, u32[]{:S(2)}, u32[]{:S(2)}) collective-permute-start(bf16[192,1536]{1,0:T(8,128)(2,1)S(1)} %broadcast_select_fusion.6), channel_id=1, source_target_pairs={{0,64},{64,128},{128,192},{192,256},{256,320},{320,384},{384,448},... | collective-permute-start | bytes 1769480 | tf_op jit(solution)/shard_map/while/body/eval_jaxpr/ppermute | solution.py:31
  249.7 4.4 %copy-start = (bf16[1536,1536]{1,0:T(8,128)(2,1)S(1)}, bf16[1536,1536]{1,0:T(8,128)(2,1)}, u32[]{:S(2)}) copy-start(bf16[1536,1536]{1,0:T(8,128)(2,1)} %get-tuple-element.1086) | copy-start | bytes 14155780 | tf_op jit(solution)/shard_map/while
  265.2 1.3 copy-start.1
  266.5 1.1 copy-start.2
  268.5 20.4 %collective-permute-start.1 = (bf16[48,3072]{1,0:T(8,128)(2,1)}, bf16[48,3072]{1,0:T(8,128)(2,1)}, u32[]{:S(2)}, u32[]{:S(2)}) collective-permute-start(bf16[48,3072]{1,0:T(8,128)(2,1)} %get-tuple-element.1018), channel_id=1, source_target_pairs={{0,1},{1,2},{2,3},{3,4},{4,5},{5,6},{6,7},{7,8},{8,9},{9,10},{10,1... | collective-permute-start | bytes 884744 | tf_op jit(solution)/shard_map/while/body/eval_jaxpr/ppermute | solution.py:22
  273.1 13.8 %collective-permute-start.2 = (bf16[48,3072]{1,0:T(8,128)(2,1)}, bf16[48,3072]{1,0:T(8,128)(2,1)}, u32[]{:S(2)}, u32[]{:S(2)}) collective-permute-start(bf16[48,3072]{1,0:T(8,128)(2,1)} %get-tuple-element.1019), channel_id=1, source_target_pairs={{1,0},{2,1},{3,2},{4,3},{5,4},{6,5},{7,6},{8,7},{9,8},{10,9},{11,1... | collective-permute-start | bytes 884744 | tf_op jit(solution)/shard_map/while/body/eval_jaxpr/ppermute | solution.py:23
  282.9 1.0 copy-start.3
  283.9 1.6 copy-start.4
  285.5 1.3 copy-start.5
  286.9 3.8 %copy-start.6 = (bf16[1,2,192,1536]{3,2,1,0:T(8,128)(2,1)}, bf16[1,2,192,1536]{3,2,1,0:T(8,128)(2,1)S(1)}, u32[]{:S(2)}) copy-start(bf16[1,2,192,1536]{3,2,1,0:T(8,128)(2,1)S(1)} %get-tuple-element.1027) | copy-start | bytes 3538948 | tf_op jit(solution)/shard_map/while
  286.9 3.8 %copy-start.8 = (f32[3,1536]{1,0:T(4,128)S(1)}, f32[3,1536]{1,0:T(4,128)}, u32[]{:S(2)}) copy-start(f32[3,1536]{1,0:T(4,128)} %copy-done.7) | copy-start | bytes 55300 | tf_op jit(solution)/shard_map/while
  286.9 3.8 %copy-start.13 = (s32[2]{0:T(128)S(1)}, s32[2]{0:T(128)}, u32[]{:S(2)}) copy-start(s32[2]{0:T(128)} %get-tuple-element.1125) | copy-start | bytes 28 | tf_op jit(solution)/shard_map/while
  290.7 10.4 %copy-start.7 = (f32[3,1536]{1,0:T(4,128)}, f32[3,1536]{1,0:T(4,128)S(1)}, u32[]{:S(2)}) copy-start(f32[3,1536]{1,0:T(4,128)S(1)} %get-tuple-element.1079) | copy-start | bytes 55300 | tf_op jit(solution)/shard_map/while
  290.7 15.5 %collective-permute-start = (bf16[192,1536]{1,0:T(8,128)(2,1)S(1)}, bf16[192,1536]{1,0:T(8,128)(2,1)S(1)}, u32[]{:S(2)}, u32[]{:S(2)}) collective-permute-start(bf16[192,1536]{1,0:T(8,128)(2,1)S(1)} %broadcast_select_fusion.6), channel_id=1, source_target_pairs={{0,64},{64,128},{128,192},{192,256},{256,320},{320,384},{384,448},... | collective-permute-start | bytes 1769480 | tf_op jit(solution)/shard_map/while/body/eval_jaxpr/ppermute | solution.py:31
  307.6 4.5 %copy-start = (bf16[1536,1536]{1,0:T(8,128)(2,1)S(1)}, bf16[1536,1536]{1,0:T(8,128)(2,1)}, u32[]{:S(2)}) copy-start(bf16[1536,1536]{1,0:T(8,128)(2,1)} %get-tuple-element.1086) | copy-start | bytes 14155780 | tf_op jit(solution)/shard_map/while
  323.2 1.3 copy-start.1
  324.5 1.1 copy-start.2
  326.4 22.9 %collective-permute-start.1 = (bf16[48,3072]{1,0:T(8,128)(2,1)}, bf16[48,3072]{1,0:T(8,128)(2,1)}, u32[]{:S(2)}, u32[]{:S(2)}) collective-permute-start(bf16[48,3072]{1,0:T(8,128)(2,1)} %get-tuple-element.1018), channel_id=1, source_target_pairs={{0,1},{1,2},{2,3},{3,4},{4,5},{5,6},{6,7},{7,8},{8,9},{9,10},{10,1... | collective-permute-start | bytes 884744 | tf_op jit(solution)/shard_map/while/body/eval_jaxpr/ppermute | solution.py:22
  333.6 13.7 %collective-permute-start.2 = (bf16[48,3072]{1,0:T(8,128)(2,1)}, bf16[48,3072]{1,0:T(8,128)(2,1)}, u32[]{:S(2)}, u32[]{:S(2)}) collective-permute-start(bf16[48,3072]{1,0:T(8,128)(2,1)} %get-tuple-element.1019), channel_id=1, source_target_pairs={{1,0},{2,1},{3,2},{4,3},{5,4},{6,5},{7,6},{8,7},{9,8},{10,9},{11,1... | collective-permute-start | bytes 884744 | tf_op jit(solution)/shard_map/while/body/eval_jaxpr/ppermute | solution.py:23
  343.3 1.0 copy-start.3
  344.3 1.6 copy-start.4
  345.8 1.3 copy-start.5
  347.3 3.8 %copy-start.6 = (bf16[1,2,192,1536]{3,2,1,0:T(8,128)(2,1)}, bf16[1,2,192,1536]{3,2,1,0:T(8,128)(2,1)S(1)}, u32[]{:S(2)}) copy-start(bf16[1,2,192,1536]{3,2,1,0:T(8,128)(2,1)S(1)} %get-tuple-element.1027) | copy-start | bytes 3538948 | tf_op jit(solution)/shard_map/while
  347.3 3.8 %copy-start.8 = (f32[3,1536]{1,0:T(4,128)S(1)}, f32[3,1536]{1,0:T(4,128)}, u32[]{:S(2)}) copy-start(f32[3,1536]{1,0:T(4,128)} %copy-done.7) | copy-start | bytes 55300 | tf_op jit(solution)/shard_map/while
  347.3 3.8 %copy-start.13 = (s32[2]{0:T(128)S(1)}, s32[2]{0:T(128)}, u32[]{:S(2)}) copy-start(s32[2]{0:T(128)} %get-tuple-element.1125) | copy-start | bytes 28 | tf_op jit(solution)/shard_map/while
Sparse Core Ops, SparseCore 0:
  10.7 191.0 all-gather.2
where the time goes:
time: 361 us; the launch traced here: 358 us
  waiting for transfers between devices  191 us (53%)
  local copies, waits for them, and re-layouts  63.1 us (17%)
  starting transfers between devices  32 us (9%)
  matrix products  28.3 us (8%)
  other arithmetic  23.6 us (7%)
  between operations  13.5 us (4%)
  loops' own time  6.89 us (2%)
    all_gather x1, waiting for transfers between devices, shards(): gathered = lax.all_gather(projection[0], 'tile', axis=2, tiled=True)  180 us
    unnamed x13, local copies, waits for them, and re-layouts  23.4 us
    ppermute x3, starting transfers between devices, with_halo(): before = lax.ppermute(last, axis, up)  13.7 us
    ppermute x3, starting transfers between devices, with_halo(): after = lax.ppermute(first, axis, down)  12.6 us
    squeeze x1, local copies, waits for them, and re-layouts, shards(): query_weight = gathered[0]  10.8 us
    ppermute x2, waiting for transfers between devices, from_behind(): lax.ppermute(value, axis, [(source, source + steps) for source in range(f...  10.6 us
    dot_general x2, matrix products, keys_values(): key_rows = jnp.dot(hidden, key_weight, preferred_element_type=jnp.float32)  9.74 us
    dot_general x2, matrix products, keys_values(): jnp.dot(hidden, value_weight, preferred_element_type=jnp.float32)  8.88 us
  transfers between devices with their start and end apart: 9, of which 3 were waited for; matrix products, arithmetic and copies ran while one was open for 18% of the time, Pallas kernels for 0%

commit v1 on v0

v1 whole, which is shorter than its diff:
```python
import math

import jax
import jax.numpy as jnp
from jax import lax
from jax.experimental import pallas as pl
from jax.experimental.pallas import tpu as pltpu
from jax.sharding import PartitionSpec as P

HEADS = 12
FEAT = 1536
TILE = 192
RIM = 48
PLANES = 16
SECTIONS = 8
TILES = 64
COLS = 24
GROUPS = 4
WIDE = FEAT // GROUPS
HEAD = FEAT // HEADS
WINDOW = 2 * TILE + 2 * RIM
EPS = 1e-06
MESH = pl.DeviceIdType.MESH
NT = (((1,), (1,)), ((), ()))


def kernel(
    x_hbm, stale_hbm, proj_hbm, mod_ref, pattern_ref, order_ref, out_ref,
    w, dense, xb, st, hidden, q, kv, o, rs, sl, su, fl, fu,
    loc_sem, zs, zr, xs, xr, d1s, d1r, d2s, d2r, rim_s, rim_r, fr_s, fr_r, str_s, str_r,
):
    section = lax.axis_index("section")
    tile = lax.axis_index("tile")
    z = tile // 4
    xh = (tile // 2) % 2
    c = tile % 2
    u = xh * 2 + c
    up = (1 - xh) * 2 + c

    def plane(d):
        return (z + d + PLANES) % PLANES

    def at_tile(t):
        return (section, t)

    z_dev = (
        at_tile(((z + 1) % PLANES) * 4 + u),
        at_tile(((z + PLANES - 1) % PLANES) * 4 + u),
    )
    x_dev = at_tile(z * 4 + up)
    sib = at_tile(z * 4 + xh * 2 + (1 - c))
    tile_hi = at_tile((tile + 1) % TILES)
    tile_lo = at_tile((tile + TILES - 1) % TILES)
    sec_hi = ((section + 1) % SECTIONS, tile)
    sec_lo = ((section + SECTIONS - 1) % SECTIONS, tile)

    own_w = pltpu.make_async_copy(proj_hbm, w.at[z, u], loc_sem.at[0])
    own_w.start()
    x_loads = [
        pltpu.make_async_copy(x_hbm.at[:, pl.ds(g * WIDE, WIDE)], xb.at[g], loc_sem.at[1 + g])
        for g in range(GROUPS)
    ]
    st_loads = [
        pltpu.make_async_copy(
            stale_hbm.at[:, pl.ds((k * GROUPS + g) * WIDE, WIDE)], st.at[g, k],
            loc_sem.at[5 + 2 * g + k],
        )
        for g in range(GROUPS)
        for k in range(2)
    ]
    for cp in x_loads + st_loads:
        cp.start()

    bar = pltpu.get_barrier_semaphore()
    peers = (z_dev[0], z_dev[1], x_dev, sib, tile_hi, tile_lo, sec_hi, sec_lo)
    for dev in peers:
        pl.semaphore_signal(bar, inc=1, device_id=dev, device_id_type=MESH)
    pl.semaphore_wait(bar, len(peers))

    def remote(src, dst, s, r, dev):
        return pltpu.make_async_remote_copy(
            src_ref=src, dst_ref=dst, send_sem=s, recv_sem=r, device_id=dev, device_id_type=MESH
        )

    def z_copy(part, way, p):
        if part == 0:
            ref = w.at[p, u, pl.ds(0, 2)]
        elif part == 1:
            ref = w.at[p, u, 2]
        else:
            ref = w.at[p, up, 2]
        return remote(ref, ref, zs.at[part, way, p], zr.at[part, p], z_dev[way])

    def z_wait(part, p):
        z_copy(part, 0, p).wait_recv()

    def x_copy(p):
        ref = w.at[p, u, pl.ds(0, 2)]
        return remote(ref, ref, xs.at[p], xr.at[p], x_dev)

    def x_own():
        ref = w.at[z, u]
        return remote(ref, ref, xs.at[z], xr.at[z], x_dev)

    def d1_copy(p):
        ref = w.at[p, u]
        return remote(ref, ref, d1s.at[p], d1r.at[p], sib)

    def d2_copy(p):
        ref = w.at[p, up]
        return remote(ref, ref, d2s.at[p], d2r.at[p], sib)

    own_w.wait()
    x_own().start()
    for way in range(2):
        z_copy(0, way, z).start()
    for way in range(2):
        z_copy(1, way, z).start()
    d1_copy(z).start()

    for cp in st_loads:
        cp.wait()
    rim_up = remote(st.at[:, :, pl.ds(0, RIM), :], su, rim_s.at[0], rim_r.at[0], tile_lo)
    rim_down = remote(
        st.at[:, :, pl.ds(2 * TILE - RIM, RIM), :], sl, rim_s.at[1], rim_r.at[1], tile_hi
    )

    parity = section % 2
    first = order_ref[0:1, 0:1]
    second = order_ref[0:1, 1:2]
    j0 = jnp.where(parity == 0, first, second)
    has_lo = jnp.where(tile > 0, 1, 0)
    has_hi = jnp.where(tile < TILES - 1, 1, 0)

    def pick(flag, yes, no):
        on = jnp.broadcast_to(flag, yes.shape) > 0
        return jnp.where(on, yes.astype(jnp.float32), no.astype(jnp.float32))

    def mask_of(j):
        def mark(slot):
            one, two = pattern_ref[0:1, slot : slot + 1], pattern_ref[1:2, slot : slot + 1]
            return one + j * (two - one)

        one, two = mark(1), mark(2)
        spans = (
            (one + j0 * (two - one), TILE),
            (two + j0 * (one - two), TILE),
            (mark(0) * has_lo, RIM),
            (mark(3) * has_hi, RIM),
        )
        lane = lax.broadcasted_iota(jnp.int32, (1, WINDOW), 1)
        marks = jnp.zeros((1, WINDOW), jnp.int32)
        start = 0
        for value, width in spans:
            inside = (lane >= start) & (lane < start + width)
            marks = jnp.where(inside, jnp.broadcast_to(value, marks.shape), marks)
            start += width
        return jnp.where(marks > 0, 1.0, 0.0)

    def tile_rows(ref, g, j):
        return pick(j, ref[g, TILE : 2 * TILE, :], ref[g, 0:TILE, :])

    def stale_other(g, n):
        one, two = st[g, n, 0:TILE, :], st[g, n, TILE : 2 * TILE, :]
        return pick(j0, one, two).astype(jnp.bfloat16)

    def modulate(parts):
        total = jnp.zeros((TILE, 1), jnp.float32)
        for part in parts:
            values = part().astype(jnp.float32)
            total = total + jnp.sum(values * values, axis=1, keepdims=True)
        inv = lax.rsqrt(total * (1.0 / FEAT) + EPS)
        for g, part in enumerate(parts):
            cols = pl.ds(g * WIDE, WIDE)
            normed = part().astype(jnp.float32) * inv
            hidden[:, cols] = (
                (1.0 + mod_ref[1:2, cols]) * normed + mod_ref[0:1, cols]
            ).astype(jnp.bfloat16)

    def head_norm(rows):
        parts = []
        for h in range(WIDE // HEAD):
            one = rows[:, h * HEAD : (h + 1) * HEAD]
            mean = jnp.mean(one * one, axis=1, keepdims=True)
            parts.append(one * lax.rsqrt(mean + EPS))
        return jnp.concatenate(parts, axis=1).astype(jnp.bfloat16)

    def project(turn, g):
        rows = hidden[...]
        for m in range(3):
            weight = dense[g, m].reshape(WIDE, FEAT)
            res = lax.dot_general(rows, weight, NT, preferred_element_type=jnp.float32)
            if m == 0:
                q[g] = head_norm(res)
            elif m == 1:
                kv[turn, g, 0] = head_norm(res)
            else:
                kv[turn, g, 1] = res.astype(jnp.bfloat16)

    def attend(g, mask, other, low, high, stream, turn):
        def window(k):
            return jnp.concatenate([kv[0, g, k], other(k), low(k), high(k)], axis=0)

        keys = window(0)
        values = window(1)
        queries = q[g]
        outs = []
        for h in range(WIDE // HEAD):
            cols = slice(h * HEAD, (h + 1) * HEAD)
            scores = lax.dot_general(
                queries[:, cols], keys[:, cols], NT, preferred_element_type=jnp.float32
            ) * (1.0 / math.sqrt(HEAD))
            unnormed = jnp.exp(scores) * mask
            total = jnp.sum(unnormed, axis=1, keepdims=True)
            weights = (unnormed / total).astype(jnp.bfloat16)
            outs.append(jnp.dot(weights, values[:, cols], preferred_element_type=jnp.float32))
        attended = jnp.concatenate(outs, axis=1)
        gate = mod_ref[2:3, pl.ds(pl.multiple_of(g * WIDE, WIDE), WIDE)]
        o[turn, g] = (stream.astype(jnp.float32) + gate * attended).astype(jnp.bfloat16)

    def lay_out(p):
        d1_copy(p).wait_recv()
        d2_copy(p).wait_recv()
        for m in range(3):
            parts = [w[p, v, m].astype(jnp.float32) for v in range(4)]
            dense[p // 4, m, p % 4] = jnp.concatenate(parts, axis=0).astype(jnp.bfloat16)

    def rim_fresh(g):
        up_copy = remote(
            kv.at[0, g, :, pl.ds(0, RIM), :], fu.at[g], fr_s.at[0, g], fr_r.at[0, g], tile_lo
        )
        down_copy = remote(
            kv.at[0, g, :, pl.ds(TILE - RIM, RIM), :], fl.at[g], fr_s.at[1, g], fr_r.at[1, g],
            tile_hi,
        )
        return up_copy, down_copy

    def stream_copy(g):
        return remote(o.at[0, g], rs.at[g], str_s.at[g], str_r.at[g], sec_hi)

    near = jnp.where(z % 4 < 2, GROUPS - 1, 1)

    def group_at(k):
        base = z // 4
        step = jnp.where(k == 0, 0, jnp.where(k == 1, near, jnp.where(k == 2, GROUPS - near, 2)))
        return (base + step) % GROUPS

    def first_turn(k):
        g = group_at(k)
        project(0, g)
        for cp in rim_fresh(g):
            cp.start()
        attend(
            g, mask_of(j0), lambda n: stale_other(g, n), lambda n: sl[g, n],
            lambda n: su[g, n], tile_rows(xb, g, j0), 0,
        )
        stream_copy(g).start()

    x_own().wait_recv()
    for way in range(2):
        z_copy(2, way, z).start()
    d2_copy(z).start()
    rim_up.start()
    rim_down.start()

    for cp in x_loads:
        cp.wait()
    modulate([lambda g=g: tile_rows(xb, g, j0) for g in range(GROUPS)])
    rim_up.wait_recv()
    rim_down.wait_recv()

    def ring_step(s, carry):
        before = plane(-s)
        after = plane(s)

        @pl.when(s <= 8)
        def _():
            z_wait(0, before)

            @pl.when(s <= 7)
            def _():
                z_copy(0, 0, before).start()

            x_copy(before).start()

        @pl.when(s <= 7)
        def _():
            z_wait(0, after)

            @pl.when(s <= 6)
            def _():
                z_copy(0, 1, after).start()

            x_copy(after).start()

        @pl.when(s >= 2)
        def _():
            p = plane(1 - s)
            x_copy(p).wait_recv()
            d2_copy(p).start()

        @pl.when((s >= 2) & (s <= 8))
        def _():
            p = plane(s - 1)
            x_copy(p).wait_recv()
            d2_copy(p).start()

        @pl.when(s <= 7)
        def _():
            for part in (1, 2):
                z_wait(part, before)

                @pl.when(s <= 6)
                def _():
                    z_copy(part, 0, before).start()

            d1_copy(before).start()

        @pl.when(s <= 8)
        def _():
            for part in (1, 2):
                z_wait(part, after)

                @pl.when(s <= 7)
                def _():
                    z_copy(part, 1, after).start()

            d1_copy(after).start()

        lay_out(plane(1 - s))

        @pl.when((s >= 2) & (s <= 8))
        def _():
            lay_out(plane(s - 1))

        @pl.when((s == 4) | (s == 6) | (s >= 8))
        def _():
            first_turn(jnp.where(s == 9, 3, (s - 4) // 2))

        return carry

    lax.fori_loop(1, 10, ring_step, 0)

    for g in range(GROUPS):
        stream_copy(g).wait_recv()
    is_first = section == 0

    def second_stream(g):
        return jnp.where(is_first, tile_rows(xb, g, 1 - j0), rs[g].astype(jnp.float32))

    modulate([lambda g=g: second_stream(g) for g in range(GROUPS)])
    for g in range(GROUPS):
        for cp in rim_fresh(g):
            cp.wait_recv()

    def second_turn(g, carry):
        project(1, g)
        attend(
            g, mask_of(1 - j0), lambda n: kv[1, g, n],
            lambda n: pick(j0, fl[g, n], sl[g, n]).astype(jnp.bfloat16),
            lambda n: pick(j0, su[g, n], fu[g, n]).astype(jnp.bfloat16),
            second_stream(g), 1,
        )
        return carry

    lax.fori_loop(0, GROUPS, second_turn, 0)
    for g in range(GROUPS):
        cols = pl.ds(g * WIDE, WIDE)
        out_ref[pl.ds(0, TILE), cols] = pick(j0, o[1, g], o[0, g]).astype(jnp.bfloat16)
        out_ref[pl.ds(TILE, TILE), cols] = pick(j0, o[0, g], o[1, g]).astype(jnp.bfloat16)

    x_own().wait_send()
    rim_up.wait_send()
    rim_down.wait_send()
    for part in range(3):
        for way in range(2):
            z_copy(part, way, z).wait_send()
    d1_copy(z).wait_send()
    d2_copy(z).wait_send()
    for g in range(GROUPS):
        for cp in rim_fresh(g):
            cp.wait_send()
        stream_copy(g).wait_send()

    def drain(s, carry):
        before = plane(-s)
        after = plane(s)
        z_copy(0, 0, before).wait_send()
        x_copy(before).wait_send()
        d1_copy(before).wait_send()
        d2_copy(before).wait_send()
        for part in (1, 2):
            z_copy(part, 1, after).wait_send()

        @pl.when(s <= 6)
        def _():
            z_copy(0, 1, after).wait_send()
            for part in (1, 2):
                z_copy(part, 0, before).wait_send()

        x_copy(after).wait_send()
        d1_copy(after).wait_send()
        d2_copy(after).wait_send()
        return carry

    lax.fori_loop(1, 8, drain, 0)
    far = plane(8)
    x_copy(far).wait_send()
    d1_copy(far).wait_send()
    d2_copy(far).wait_send()


def shards(block_inputs, stale_kv, projection, modulation, pattern, order):
    dma = pltpu.SemaphoreType.DMA
    vmem = pltpu.VMEM
    bf16 = jnp.bfloat16
    out = pl.pallas_call(
        kernel,
        out_shape=jax.ShapeDtypeStruct((2 * TILE, FEAT), bf16),
        in_specs=[pl.BlockSpec(memory_space=pl.ANY)] * 3
        + [pl.BlockSpec(memory_space=pltpu.VMEM)] * 3,
        out_specs=pl.BlockSpec(memory_space=pltpu.VMEM),
        scratch_shapes=[
            vmem((PLANES, 4, 3, COLS, FEAT), bf16),
            vmem((GROUPS, 3, 4, 4 * COLS, FEAT), bf16),
            vmem((GROUPS, 2 * TILE, WIDE), bf16),
            vmem((GROUPS, 2, 2 * TILE, WIDE), bf16),
            vmem((TILE, FEAT), bf16),
            vmem((GROUPS, TILE, WIDE), bf16),
            vmem((2, GROUPS, 2, TILE, WIDE), bf16),
            vmem((2, GROUPS, TILE, WIDE), bf16),
            vmem((GROUPS, TILE, WIDE), bf16),
            vmem((GROUPS, 2, RIM, WIDE), bf16),
            vmem((GROUPS, 2, RIM, WIDE), bf16),
            vmem((GROUPS, 2, RIM, WIDE), bf16),
            vmem((GROUPS, 2, RIM, WIDE), bf16),
            dma((13,)),
            dma((3, 2, PLANES)),
            dma((3, PLANES)),
            dma((PLANES,)),
            dma((PLANES,)),
            dma((PLANES,)),
            dma((PLANES,)),
            dma((PLANES,)),
            dma((PLANES,)),
            dma((2,)),
            dma((2,)),
            dma((2, GROUPS)),
            dma((2, GROUPS)),
            dma((GROUPS,)),
            dma((GROUPS,)),
        ],
        compiler_params=pltpu.CompilerParams(
            collective_id=0, has_side_effects=True, vmem_limit_bytes=58 * 2**20
        ),
        name="blocks",
    )(
        block_inputs[0],
        stale_kv[0],
        jnp.swapaxes(projection[0], 1, 2),
        modulation[0],
        pattern,
        order.reshape(1, 2),
    )
    return out[None]


def solution(mesh):
    placed = (
        P("section", "tile", None),
        P("section", "tile", None),
        P("section", None, None, "tile"),
        P("section", None, None),
        P("tile", None),
        P(),
    )
    return jax.shard_map(
        shards, mesh=mesh, in_specs=placed, out_specs=P("section", "tile", None), check_vma=False
    )
```

time: 361 us -> 121 us (0.34)
  waiting for transfers between devices: 191 us -> 0 us
  Pallas kernels: 0 us -> 117 us
  local copies, waits for them, and re-layouts: 63.1 us -> 3.7 us
  starting transfers between devices: 32 us -> 0 us
  matrix products: 28.3 us -> 0 us
  other arithmetic: 23.6 us -> 0 us
  between operations: 13.5 us -> 0.01 us
  loops' own time: 6.89 us -> 0 us
    all_gather x1 -> x0, waiting for transfers between devices: 180 us -> none  [shards(): gathered = lax.all_gather(projection[0], 'tile', axis=2, tiled=True)]
    pallas_call x0 -> x1, Pallas kernels: none -> 117 us  [shards(): pl.pallas_call(kernel, out_shape=jax.ShapeDtypeStruct((2 * TILE, FEAT), b...]
    ppermute x8 -> x0, starting transfers between devices: 32 us -> none  [the longest x3 13.7 us: with_halo(): before = lax.ppermute(last, axis, up)]
    dot_general x10 -> x0, matrix products: 28.3 us -> none  [the longest x2 9.74 us: keys_values(): key_rows = jnp.dot(hidden, key_weight, preferred_element_type=jnp.float32)]
    unnamed x13 -> x2, local copies, waits for them, and re-layouts: 23.4 us -> 3.7 us
    squeeze x1 -> x0, local copies, waits for them, and re-layouts: 10.8 us -> none  [shards(): query_weight = gathered[0]]
    ppermute x8 -> x0, waiting for transfers between devices: 10.6 us -> none  [the longest x2 10.6 us: from_behind(): lax.ppermute(value, axis, [(source, source + steps) for source in range(f...]
    slice x7 -> x0, local copies, waits for them, and re-layouts: 10.3 us -> none  [the longest x4 6.05 us: attend(): key_heads = window[:, :feat_width].reshape(-1, head_count, head_width)]
  transfers between devices with their start and end apart: 9 -> 0, of which waited for: 3 -> 0; matrix products, arithmetic and copies ran while one was open for 18% -> 0% of each run, Pallas kernels for 0% -> 0%
where the time goes in v1:
time: 121 us
  Pallas kernels  117 us (97%)
  local copies, waits for them, and re-layouts  3.7 us (3%)
    pallas_call x1, Pallas kernels, shards(): pl.pallas_call(kernel, out_shape=jax.ShapeDtypeStruct((2 * TILE, FEAT), b...  117 us
    unnamed x2, local copies, waits for them, and re-layouts  3.7 us

profile of v1, /device:TPU:1, one launch (start us, length us, event | category | flops | bytes accessed | tf_op | source)
XLA Modules:
  0.0 120.6 jit_solution(14841416919518729746)
XLA Ops:
  0.0 1.3 %copy.9 = f32[1,3,1536]{2,1,0:T(4,128)} copy(f32[1,3,1536]{2,0,1:T(1,128)} %param.9) | data formatting | bytes 36864
  1.3 116.9 %blocks.1 = bf16[384,1536]{1,0:T(8,128)(2,1)} custom-call(bf16[384,1536]{1,0:T(8,128)(2,1)} %bitcast.12, bf16[384,3072]{1,0:T(8,128)(2,1)} %bitcast.11, bf16[3,24,1536]{2,1,0:T(8,128)(2,1)} %bitcast.13, f32[3,1536]{1,0:T(4,128)} %bitcast.14, s32[2,4]{1,0:T(2,128)} %pattern_ref.1, s32[1,2]{1,0:T(1,128)} %bitcast.15), custom_call_target="tpu_custom_call" | custom-call | tf_op jit(solution)/shard_map/blocks/pallas_call | solution.py:417
  118.2 2.4 %copy.11 = bf16[1,384,1536]{2,1,0:T(8,128)(2,1)} copy(bf16[1,384,1536]{2,1,0:T(8,128)(2,1)} %bitcast.10) | data formatting | bytes 2359296

commit v2 on v1

v2 whole, which is shorter than its diff:
```python
import math

import jax
import jax.numpy as jnp
from jax import lax
from jax.experimental import pallas as pl
from jax.experimental.pallas import tpu as pltpu
from jax.sharding import PartitionSpec as P

HEADS = 12
FEAT = 1536
TILE = 192
RIM = 48
PLANES = 16
SECTIONS = 8
TILES = 64
COLS = 24
GROUPS = 4
WIDE = FEAT // GROUPS
HEAD = FEAT // HEADS
WINDOW = 2 * TILE + 2 * RIM
DUP = 768
EPS = 1e-06
MESH = pl.DeviceIdType.MESH
NT = (((1,), (1,)), ((), ()))
SCALE = math.log2(math.e) / math.sqrt(HEAD)


def kernel(
    x_hbm, stale_hbm, proj_hbm, mod_hbm, pattern_ref, order_ref, out_ref,
    w, dense, xb, st, hidden, q, kv, o, rs, sl, su, xl, xu, fr, marks, mod_ref,
    loc_sem, zs, zr, xs, xr, d1s, d1r, d2s, d2r, rim_s, rim_r, str_s, str_r, out_sem,
):
    section = lax.axis_index("section")
    tile = lax.axis_index("tile")
    z = tile // 4
    xh = (tile // 2) % 2
    c = tile % 2
    u = xh * 2 + c
    up = (1 - xh) * 2 + c

    def plane(d):
        return (z + d + PLANES) % PLANES

    def at_tile(t):
        return (section, t)

    z_dev = (
        at_tile(((z + 1) % PLANES) * 4 + u),
        at_tile(((z + PLANES - 1) % PLANES) * 4 + u),
    )
    x_dev = at_tile(z * 4 + up)
    sib = at_tile(z * 4 + xh * 2 + (1 - c))
    tile_hi = at_tile((tile + 1) % TILES)
    tile_lo = at_tile((tile + TILES - 1) % TILES)
    sec_hi = ((section + 1) % SECTIONS, tile)
    sec_lo = ((section + SECTIONS - 1) % SECTIONS, tile)

    own_w = pltpu.make_async_copy(proj_hbm, w.at[z, u], loc_sem.at[0])
    own_w.start()
    x_loads = [
        pltpu.make_async_copy(x_hbm.at[:, pl.ds(g * WIDE, WIDE)], xb.at[g], loc_sem.at[1 + g])
        for g in range(GROUPS)
    ]
    st_loads = [
        pltpu.make_async_copy(
            stale_hbm.at[:, pl.ds((k * GROUPS + g) * WIDE, WIDE)], st.at[g, k],
            loc_sem.at[5 + 2 * g + k],
        )
        for g in range(GROUPS)
        for k in range(2)
    ]
    mod_loads = [
        pltpu.make_async_copy(mod_hbm.at[m], mod_ref.at[pl.ds(m, 1)], loc_sem.at[13 + m])
        for m in range(3)
    ]
    for cp in x_loads + st_loads + mod_loads:
        cp.start()

    bar = pltpu.get_barrier_semaphore()
    peers = (z_dev[0], z_dev[1], x_dev, sib, tile_hi, tile_lo, sec_hi, sec_lo)
    for dev in peers:
        pl.semaphore_signal(bar, inc=1, device_id=dev, device_id_type=MESH)
    pl.semaphore_wait(bar, len(peers))

    def remote(src, dst, s, r, dev):
        return pltpu.make_async_remote_copy(
            src_ref=src, dst_ref=dst, send_sem=s, recv_sem=r, device_id=dev, device_id_type=MESH
        )

    def z_copy(part, way, p):
        if part == 0:
            ref = w.at[p, u, pl.ds(0, 2)]
        elif part == 1:
            ref = w.at[p, u, 2]
        elif part == 2:
            ref = w.at[p, up, 2]
        else:
            ref = w.at[p, up, 1, :, pl.ds(0, DUP)]
        return remote(ref, ref, zs.at[part, way, p], zr.at[part, p], z_dev[way])

    def z_wait(part, p):
        z_copy(part, 0, p).wait_recv()

    def x_copies(p):
        refs = (w.at[p, u, 0], w.at[p, u, 1, :, pl.ds(DUP, FEAT - DUP)])
        return [
            remote(ref, ref, xs.at[i, p], xr.at[i, p], x_dev) for i, ref in enumerate(refs)
        ]

    def x_own():
        refs = (w.at[z, u, 0], w.at[z, u, pl.ds(1, 2)])
        return [
            remote(ref, ref, xs.at[i, z], xr.at[i, z], x_dev) for i, ref in enumerate(refs)
        ]

    def x_start(p):
        for cp in x_copies(p):
            cp.start()

    def x_wait(p):
        for cp in x_copies(p):
            cp.wait_recv()

    def x_drain(p):
        for cp in x_copies(p):
            cp.wait_send()

    def d1_copy(p):
        ref = w.at[p, u]
        return remote(ref, ref, d1s.at[p], d1r.at[p], sib)

    def d2_copy(p):
        ref = w.at[p, up]
        return remote(ref, ref, d2s.at[p], d2r.at[p], sib)

    own_w.wait()
    x_own()[1].start()
    x_own()[0].start()
    for part in (0, 1):
        for way in range(2):
            z_copy(part, way, z).start()
    d1_copy(z).start()

    head_rows = pl.ds(0, RIM)
    tail_rows = pl.ds(2 * TILE - RIM, RIM)
    rims = [
        remote(st.at[:, :, head_rows, :], su, rim_s.at[0], rim_r.at[0], tile_lo),
        remote(st.at[:, :, tail_rows, :], sl, rim_s.at[1], rim_r.at[1], tile_hi),
        remote(xb.at[:, head_rows, :], xu, rim_s.at[2], rim_r.at[2], tile_lo),
        remote(xb.at[:, tail_rows, :], xl, rim_s.at[3], rim_r.at[3], tile_hi),
    ]

    parity = section % 2
    first = order_ref[0:1, 0:1]
    second = order_ref[0:1, 1:2]
    j0 = jnp.where(parity == 0, first, second)
    has_lo = jnp.where(tile > 0, 1, 0)
    has_hi = jnp.where(tile < TILES - 1, 1, 0)

    def pick(flag, yes, no):
        on = jnp.broadcast_to(flag, yes.shape) > 0
        return jnp.where(on, yes.astype(jnp.float32), no.astype(jnp.float32))

    def set_marks(turn, j):
        def mark(slot):
            one, two = pattern_ref[0:1, slot : slot + 1], pattern_ref[1:2, slot : slot + 1]
            return one + j * (two - one)

        one, two = mark(1), mark(2)
        spans = (
            (one + j0 * (two - one), TILE),
            (two + j0 * (one - two), TILE),
            (mark(0) * has_lo, RIM),
            (mark(3) * has_hi, RIM),
        )
        start = 0
        for value, width in spans:
            on = jnp.broadcast_to(value, (width, HEAD)) > 0
            marks[turn, pl.ds(start, width), :] = jnp.where(on, 1.0, 0.0).astype(jnp.bfloat16)
            start += width

    def tile_rows(ref, g, j):
        return pick(j, ref[g, TILE : 2 * TILE, :], ref[g, 0:TILE, :])

    def stale_other(g, n):
        one, two = st[g, n, 0:TILE, :], st[g, n, TILE : 2 * TILE, :]
        return pick(j0, one, two).astype(jnp.bfloat16)

    def modulate(parts, start, count):
        total = jnp.zeros((count, 1), jnp.float32)
        for part in parts:
            values = part()
            total = total + jnp.sum(values * values, axis=1, keepdims=True)
        inv = lax.rsqrt(total * (1.0 / FEAT) + EPS)
        for g, part in enumerate(parts):
            cols = pl.ds(g * WIDE, WIDE)
            normed = part() * inv
            hidden[pl.ds(start, count), cols] = (
                (1.0 + mod_ref[1:2, cols]) * normed + mod_ref[0:1, cols]
            ).astype(jnp.bfloat16)

    def head_norm(rows, factor):
        parts = []
        for h in range(WIDE // HEAD):
            one = rows[:, h * HEAD : (h + 1) * HEAD]
            mean = jnp.mean(one * one, axis=1, keepdims=True)
            parts.append(one * (lax.rsqrt(mean + EPS) * factor))
        return jnp.concatenate(parts, axis=1).astype(jnp.bfloat16)

    def project(turn, g):
        count = TILE + RIM if turn == 0 else TILE
        rows = hidden[pl.ds(0, count), :]
        for m in range(3):
            weight = dense[g, m].reshape(WIDE, FEAT)
            res = lax.dot_general(
                rows if m else rows[0:TILE], weight, NT, preferred_element_type=jnp.float32
            )
            low = head_norm(res, 1.0 if m else SCALE) if m < 2 else res.astype(jnp.bfloat16)
            if m == 0:
                q[g] = low
                continue
            kv[turn, g, m - 1] = low[0:TILE]
            if turn == 0:
                fr[g, m - 1] = low[TILE:count]

    def attend(g, turn, other, low, high, stream, ready):
        def window(k):
            return jnp.concatenate([kv[0, g, k], other(k), low(k), high(k)], axis=0)

        keys = window(0)
        values = window(1)
        queries = q[g]
        mark = marks[turn]
        gate = mod_ref[2:3, pl.ds(pl.multiple_of(g * WIDE, WIDE), WIDE)]
        for h in range(WIDE // HEAD):
            cols = slice(h * HEAD, (h + 1) * HEAD)
            scores = lax.dot_general(
                queries[:, cols], keys[:, cols], NT, preferred_element_type=jnp.float32
            )
            unnormed = jnp.exp2(scores).astype(jnp.bfloat16)
            marked = jnp.concatenate([values[:, cols] * mark, mark], axis=1)
            both = jnp.dot(unnormed, marked, preferred_element_type=jnp.float32)
            attended = both[:, :HEAD] / both[:, HEAD:]
            o[turn, g, :, cols] = (stream[:, cols] + gate[:, cols] * attended).astype(jnp.bfloat16)
            ready(g, h)
        out_copy(turn, g).start()

    def out_copy(turn, g):
        cols = pl.ds(pl.multiple_of(g * WIDE, WIDE), WIDE)
        return pltpu.make_async_copy(o.at[turn, g], out_ref.at[turn, :, cols], out_sem.at[turn, g])

    def lay_out(p):
        d1_copy(p).wait_recv()
        d2_copy(p).wait_recv()
        for m in range(3):
            parts = [w[p, v, m].astype(jnp.float32) for v in range(4)]
            dense[p // 4, m, p % 4] = jnp.concatenate(parts, axis=0).astype(jnp.bfloat16)

    def stream_copy(g, h):
        cols = pl.ds(h * HEAD, HEAD)
        return remote(
            o.at[0, g, :, cols], rs.at[0, g, :, cols], str_s.at[g, h], str_r.at[g, h], sec_hi
        )

    def send_stream(g, h):
        stream_copy(g, h).start()

    each_part = [(g, h) for g in range(GROUPS) for h in range(WIDE // HEAD)]

    near = jnp.where(z % 4 < 2, GROUPS - 1, 1)

    def group_at(k):
        base = z // 4
        step = jnp.where(k == 0, 0, jnp.where(k == 1, near, jnp.where(k == 2, GROUPS - near, 2)))
        return (base + step) % GROUPS

    def first_turn(k):
        g = group_at(k)
        project(0, g)
        attend(
            g, 0, lambda n: stale_other(g, n), lambda n: sl[g, n], lambda n: su[g, n],
            tile_rows(xb, g, j0), send_stream,
        )

    x_own()[1].wait_recv()
    for part in (2, 3):
        for way in range(2):
            z_copy(part, way, z).start()
    x_own()[0].wait_recv()
    d2_copy(z).start()

    def prepare():
        for cp in x_loads + st_loads + mod_loads:
            cp.wait()
        for cp in rims:
            cp.start()
        modulate([lambda g=g: tile_rows(xb, g, j0) for g in range(GROUPS)], 0, TILE)
        set_marks(0, j0)
        set_marks(1, 1 - j0)

        @pl.when(section == 0)
        def _():
            for g in range(GROUPS):
                rs[1, g] = tile_rows(xb, g, 1 - j0).astype(jnp.bfloat16)

    def neighbours():
        for cp in rims:
            cp.wait_recv()
        modulate([lambda g=g: pick(j0, xl[g], xu[g]) for g in range(GROUPS)], TILE, RIM)

    def ring_step(s, carry):
        before = plane(-s)
        after = plane(s)

        @pl.when(s <= 8)
        def _():
            z_wait(0, before)

            @pl.when(s <= 7)
            def _():
                z_copy(0, 0, before).start()

            x_start(before)

        @pl.when(s <= 7)
        def _():
            z_wait(0, after)

            @pl.when(s <= 6)
            def _():
                z_copy(0, 1, after).start()

            x_start(after)

        @pl.when(s >= 2)
        def _():
            p = plane(1 - s)
            x_wait(p)
            d2_copy(p).start()

        @pl.when((s >= 2) & (s <= 8))
        def _():
            p = plane(s - 1)
            x_wait(p)
            d2_copy(p).start()

        @pl.when(s <= 7)
        def _():
            for part in (1, 2, 3):
                z_wait(part, before)

                @pl.when(s <= 6)
                def _():
                    z_copy(part, 0, before).start()

            d1_copy(before).start()

        @pl.when(s <= 8)
        def _():
            for part in (1, 2, 3):
                z_wait(part, after)

                @pl.when(s <= 7)
                def _():
                    z_copy(part, 1, after).start()

            d1_copy(after).start()

        @pl.when(s == 1)
        def _():
            prepare()

        @pl.when(s == 3)
        def _():
            neighbours()

        lay_out(plane(1 - s))

        @pl.when((s >= 2) & (s <= 8))
        def _():
            lay_out(plane(s - 1))

        @pl.when((s == 4) | (s == 6) | (s >= 8))
        def _():
            first_turn(jnp.where(s == 9, 3, (s - 4) // 2))

        return carry

    lax.fori_loop(1, 10, ring_step, 0)

    for g, h in each_part:
        stream_copy(g, h).wait_recv()
    source = jnp.where(section == 0, 1, 0)
    modulate([lambda g=g: rs[source, g].astype(jnp.float32) for g in range(GROUPS)], 0, TILE)

    def second_turn(g, carry):
        project(1, g)
        attend(
            g, 1, lambda n: kv[1, g, n],
            lambda n: pick(j0, fr[g, n], sl[g, n]).astype(jnp.bfloat16),
            lambda n: pick(j0, su[g, n], fr[g, n]).astype(jnp.bfloat16),
            rs[source, g].astype(jnp.float32), lambda g, h: None,
        )
        return carry

    lax.fori_loop(0, GROUPS, second_turn, 0)

    for cp in x_own() + rims:
        cp.wait_send()
    for part in range(4):
        for way in range(2):
            z_copy(part, way, z).wait_send()
    d1_copy(z).wait_send()
    d2_copy(z).wait_send()
    for turn in range(2):
        for g in range(GROUPS):
            out_copy(turn, g).wait()

    for g, h in each_part:
        stream_copy(g, h).wait_send()

    def drain(s, carry):
        before = plane(-s)
        after = plane(s)
        z_copy(0, 0, before).wait_send()
        x_drain(before)
        d1_copy(before).wait_send()
        d2_copy(before).wait_send()
        for part in (1, 2, 3):
            z_copy(part, 1, after).wait_send()

        @pl.when(s <= 6)
        def _():
            z_copy(0, 1, after).wait_send()
            for part in (1, 2, 3):
                z_copy(part, 0, before).wait_send()

        x_drain(after)
        d1_copy(after).wait_send()
        d2_copy(after).wait_send()
        return carry

    lax.fori_loop(1, 8, drain, 0)
    far = plane(8)
    x_drain(far)
    d1_copy(far).wait_send()
    d2_copy(far).wait_send()


def shards(block_inputs, stale_kv, projection, modulation, pattern, order):
    dma = pltpu.SemaphoreType.DMA
    vmem = pltpu.VMEM
    bf16 = jnp.bfloat16
    out = pl.pallas_call(
        kernel,
        out_shape=jax.ShapeDtypeStruct((2, TILE, FEAT), bf16),
        in_specs=[pl.BlockSpec(memory_space=pl.ANY)] * 4
        + [pl.BlockSpec(memory_space=pltpu.VMEM)] * 2,
        out_specs=pl.BlockSpec(memory_space=pl.ANY),
        scratch_shapes=[
            vmem((PLANES, 4, 3, COLS, FEAT), bf16),
            vmem((GROUPS, 3, 4, 4 * COLS, FEAT), bf16),
            vmem((GROUPS, 2 * TILE, WIDE), bf16),
            vmem((GROUPS, 2, 2 * TILE, WIDE), bf16),
            vmem((TILE + RIM, FEAT), bf16),
            vmem((GROUPS, TILE, WIDE), bf16),
            vmem((2, GROUPS, 2, TILE, WIDE), bf16),
            vmem((2, GROUPS, TILE, WIDE), bf16),
            vmem((2, GROUPS, TILE, WIDE), bf16),
            vmem((GROUPS, 2, RIM, WIDE), bf16),
            vmem((GROUPS, 2, RIM, WIDE), bf16),
            vmem((GROUPS, RIM, WIDE), bf16),
            vmem((GROUPS, RIM, WIDE), bf16),
            vmem((GROUPS, 2, RIM, WIDE), bf16),
            vmem((2, WINDOW, HEAD), bf16),
            vmem((8, FEAT), jnp.float32),
            dma((16,)),
            dma((4, 2, PLANES)),
            dma((4, PLANES)),
            dma((2, PLANES)),
            dma((2, PLANES)),
            dma((PLANES,)),
            dma((PLANES,)),
            dma((PLANES,)),
            dma((PLANES,)),
            dma((4,)),
            dma((4,)),
            dma((GROUPS, WIDE // HEAD)),
            dma((GROUPS, WIDE // HEAD)),
            dma((2, GROUPS)),
        ],
        compiler_params=pltpu.CompilerParams(
            collective_id=0, has_side_effects=True, vmem_limit_bytes=58 * 2**20
        ),
        name="blocks",
    )(
        block_inputs[0],
        stale_kv[0],
        jnp.swapaxes(projection[0], 1, 2),
        jnp.swapaxes(modulation, 0, 1),
        pattern,
        order.reshape(1, 2),
    )
    swapped = order[lax.axis_index("section") % 2] > 0
    placed = jnp.where(swapped, out[::-1], out)
    return placed.reshape(1, 2 * TILE, FEAT)


def solution(mesh):
    placed = (
        P("section", "tile", None),
        P("section", "tile", None),
        P("section", None, None, "tile"),
        P("section", None, None),
        P("tile", None),
        P(),
    )
    return jax.shard_map(
        shards, mesh=mesh, in_specs=placed, out_specs=P("section", "tile", None), check_vma=False
    )
```

time: 121 us -> 107 us (0.88)
  Pallas kernels: 117 us -> 102 us
  other arithmetic: 0 us -> 2.91 us
  local copies, waits for them, and re-layouts: 3.7 us -> 1.24 us
    pallas_call x1, Pallas kernels: 117 us -> 102 us  [shards(): pl.pallas_call(kernel, out_shape=jax.ShapeDtypeStruct((2, TILE, FEAT), bf...]
    unnamed x2 -> x0, local copies, waits for them, and re-layouts: 3.7 us -> none
    select_n x0 -> x1, other arithmetic: none -> 2.91 us  [shards(): placed = jnp.where(swapped, out[::-1], out)]
    dynamic_slice x0 -> x1, local copies, waits for them, and re-layouts: none -> 1.24 us  [shards(): swapped = order[lax.axis_index('section') % 2] > 0]
where the time goes in v2:
time: 107 us
  Pallas kernels  102 us (95%)
  other arithmetic  2.91 us (3%)
  local copies, waits for them, and re-layouts  1.24 us (1%)
    pallas_call x1, Pallas kernels, shards(): pl.pallas_call(kernel, out_shape=jax.ShapeDtypeStruct((2, TILE, FEAT), bf...  102 us
    select_n x1, other arithmetic, shards(): placed = jnp.where(swapped, out[::-1], out)  2.91 us

profile of v2, /device:TPU:1, one launch (start us, length us, event | category | flops | bytes accessed | tf_op | source)
XLA Modules:
  0.0 106.5 jit_solution(4496372634477769261)
XLA Ops:
  0.0 1.2 %dynamic_slice.3 = s32[1]{0:T(128)} dynamic-slice(s32[2]{0:T(128)} %param.11, s32[]{:T(128)S(6)} %select_n.19), dynamic_slice_sizes={1} | dynamic-slice | bytes 12 | tf_op jit(solution)/shard_map/dynamic_slice | solution.py:505
  1.9 101.7 %blocks.1 = bf16[2,192,1536]{2,1,0:T(8,128)(2,1)} custom-call(bf16[384,1536]{1,0:T(8,128)(2,1)} %bitcast.10, bf16[384,3072]{1,0:T(8,128)(2,1)} %bitcast.9, bf16[3,24,1536]{2,1,0:T(8,128)(2,1)} %bitcast.11, f32[3,1,1536]{2,1,0:T(1,128)} %bitcast.12, s32[2,4]{1,0:T(2,128)} %pattern_ref.1, s32[1,2]{1,0:T(1,128)} %bitcast.13), custom_call_target="tpu_custom_call" | custom-call | tf_op jit(solution)/shard_map/blocks/pallas_call | solution.py:455
  103.6 2.9 %reverse_select_fusion = bf16[2,192,1536]{2,1,0:T(8,128)(2,1)} fusion(bf16[2,192,1536]{2,1,0:T(8,128)(2,1)} %blocks.1, pred[]{:T(512)} %bitcast), kind=kLoop, calls=%fused_computation | loop fusion | flops 589824 | bytes 2359297 | tf_op jit(solution)/shard_map/jit(_where)/select_n | solution.py:506

commit v3 on v2

--- a/solution.py
+++ b/solution.py
@@ -28,7 +28,7 @@
 
 def kernel(
     x_hbm, stale_hbm, proj_hbm, mod_hbm, pattern_ref, order_ref, out_ref,
-    w, dense, xb, st, hidden, q, kv, o, rs, sl, su, xl, xu, fr, marks, mod_ref,
+    w, dense, turned, stage, xb, st, hidden, q, kv, o, rs, sl, su, xl, xu, fr, marks, mod_ref,
     loc_sem, zs, zr, xs, xr, d1s, d1r, d2s, d2r, rim_s, rim_r, str_s, str_r, out_sem,
 ):
     section = lax.axis_index("section")
@@ -208,8 +208,20 @@
             parts.append(one * (lax.rsqrt(mean + EPS) * factor))
         return jnp.concatenate(parts, axis=1).astype(jnp.bfloat16)
 
-    def project(turn, g):
-        count = TILE + RIM if turn == 0 else TILE
+    def turn_weights(g):
+        for m in range(3):
+            turned[g, :, m * WIDE : (m + 1) * WIDE] = dense[g, m].reshape(WIDE, FEAT).T
+
+    def project_again(g):
+        res = jnp.dot(
+            hidden[pl.ds(0, TILE), :], turned[g], preferred_element_type=jnp.float32
+        )
+        q[g] = head_norm(res[:, 0:WIDE], SCALE)
+        kv[1, g, 0] = head_norm(res[:, WIDE : 2 * WIDE], 1.0)
+        kv[1, g, 1] = res[:, 2 * WIDE : 3 * WIDE].astype(jnp.bfloat16)
+
+    def project(g):
+        count = TILE + RIM
         rows = hidden[pl.ds(0, count), :]
         for m in range(3):
             weight = dense[g, m].reshape(WIDE, FEAT)
@@ -220,9 +232,8 @@
             if m == 0:
                 q[g] = low
                 continue
-            kv[turn, g, m - 1] = low[0:TILE]
-            if turn == 0:
-                fr[g, m - 1] = low[TILE:count]
+            kv[0, g, m - 1] = low[0:TILE]
+            fr[g, m - 1] = low[TILE:count]
 
     def attend(g, turn, other, low, high, stream, ready):
         def window(k):
@@ -244,11 +255,18 @@
             attended = both[:, :HEAD] / both[:, HEAD:]
             o[turn, g, :, cols] = (stream[:, cols] + gate[:, cols] * attended).astype(jnp.bfloat16)
             ready(g, h)
-        out_copy(turn, g).start()
-
-    def out_copy(turn, g):
+
+    def out_copy(j, g):
+        rows = pl.ds(j * TILE, TILE)
         cols = pl.ds(pl.multiple_of(g * WIDE, WIDE), WIDE)
-        return pltpu.make_async_copy(o.at[turn, g], out_ref.at[turn, :, cols], out_sem.at[turn, g])
+        return pltpu.make_async_copy(stage.at[j, g], out_ref.at[rows, cols], out_sem.at[j, g])
+
+    def put_out(g):
+        early, late = o[0, g], o[1, g]
+        stage[0, g] = pick(j0, late, early).astype(jnp.bfloat16)
+        stage[1, g] = pick(j0, early, late).astype(jnp.bfloat16)
+        for j in range(2):
+            out_copy(j, g).start()
 
     def lay_out(p):
         d1_copy(p).wait_recv()
@@ -277,7 +295,7 @@
 
     def first_turn(k):
         g = group_at(k)
-        project(0, g)
+        project(g)
         attend(
             g, 0, lambda n: stale_other(g, n), lambda n: sl[g, n], lambda n: su[g, n],
             tile_rows(xb, g, j0), send_stream,
@@ -385,23 +403,33 @@
         def _():
             first_turn(jnp.where(s == 9, 3, (s - 4) // 2))
 
+        @pl.when((s == 5) | (s == 7))
+        def _():
+            turn_weights(group_at((s - 5) // 2))
+
         return carry
 
     lax.fori_loop(1, 10, ring_step, 0)
 
+    def last_turned(k, carry):
+        turn_weights(group_at(k))
+        return carry
+
+    lax.fori_loop(2, GROUPS, last_turned, 0)
     for g, h in each_part:
         stream_copy(g, h).wait_recv()
     source = jnp.where(section == 0, 1, 0)
     modulate([lambda g=g: rs[source, g].astype(jnp.float32) for g in range(GROUPS)], 0, TILE)
 
     def second_turn(g, carry):
-        project(1, g)
+        project_again(g)
         attend(
             g, 1, lambda n: kv[1, g, n],
             lambda n: pick(j0, fr[g, n], sl[g, n]).astype(jnp.bfloat16),
             lambda n: pick(j0, su[g, n], fr[g, n]).astype(jnp.bfloat16),
             rs[source, g].astype(jnp.float32), lambda g, h: None,
         )
+        put_out(g)
         return carry
 
     lax.fori_loop(0, GROUPS, second_turn, 0)
@@ -413,9 +441,9 @@
             z_copy(part, way, z).wait_send()
     d1_copy(z).wait_send()
     d2_copy(z).wait_send()
-    for turn in range(2):
+    for j in range(2):
         for g in range(GROUPS):
-            out_copy(turn, g).wait()
+            out_copy(j, g).wait()
 
     for g, h in each_part:
         stream_copy(g, h).wait_send()
@@ -454,13 +482,15 @@
     bf16 = jnp.bfloat16
     out = pl.pallas_call(
         kernel,
-        out_shape=jax.ShapeDtypeStruct((2, TILE, FEAT), bf16),
+        out_shape=jax.ShapeDtypeStruct((2 * TILE, FEAT), bf16),
         in_specs=[pl.BlockSpec(memory_space=pl.ANY)] * 4
         + [pl.BlockSpec(memory_space=pltpu.VMEM)] * 2,
         out_specs=pl.BlockSpec(memory_space=pl.ANY),
         scratch_shapes=[
             vmem((PLANES, 4, 3, COLS, FEAT), bf16),
             vmem((GROUPS, 3, 4, 4 * COLS, FEAT), bf16),
+            vmem((GROUPS, FEAT, 3 * WIDE), bf16),
+            vmem((2, GROUPS, TILE, WIDE), bf16),
             vmem((GROUPS, 2 * TILE, WIDE), bf16),
             vmem((GROUPS, 2, 2 * TILE, WIDE), bf16),
             vmem((TILE + RIM, FEAT), bf16),
@@ -502,9 +532,7 @@
         pattern,
         order.reshape(1, 2),
     )
-    swapped = order[lax.axis_index("section") % 2] > 0
-    placed = jnp.where(swapped, out[::-1], out)
-    return placed.reshape(1, 2 * TILE, FEAT)
+    return out[None]
 
 
 def solution(mesh):

time: 107 us -> 104 us (0.972)
  other arithmetic: 2.91 us -> 0 us
  local copies, waits for them, and re-layouts: 1.24 us -> 2.36 us
    select_n x1 -> x0, other arithmetic: 2.91 us -> none  [shards(): placed = jnp.where(swapped, out[::-1], out)]
    unnamed x0 -> x1, local copies, waits for them, and re-layouts: none -> 2.36 us
    dynamic_slice x1 -> x0, local copies, waits for them, and re-layouts: 1.24 us -> none  [shards(): swapped = order[lax.axis_index('section') % 2] > 0]
where the time goes in v3:
time: 104 us; the launch traced here: 103 us
  Pallas kernels  101 us (97%)
  local copies, waits for them, and re-layouts  2.36 us (2%)
    pallas_call x1, Pallas kernels, shards(): pl.pallas_call(kernel, out_shape=jax.ShapeDtypeStruct((2 * TILE, FEAT), b...  101 us
    unnamed x1, local copies, waits for them, and re-layouts  2.36 us

profile of v3, /device:TPU:1, one launch (start us, length us, event | category | flops | bytes accessed | tf_op | source)
XLA Modules:
  0.0 103.4 jit_solution(14583202898510415748)
XLA Ops:
  0.0 101.0 %blocks.1 = bf16[384,1536]{1,0:T(8,128)(2,1)} custom-call(bf16[384,1536]{1,0:T(8,128)(2,1)} %bitcast.10, bf16[384,3072]{1,0:T(8,128)(2,1)} %bitcast.9, bf16[3,24,1536]{2,1,0:T(8,128)(2,1)} %bitcast.11, f32[3,1,1536]{2,1,0:T(1,128)} %bitcast.12, s32[2,4]{1,0:T(2,128)} %pattern_ref.1, s32[1,2]{1,0:T(1,128)} %bitcast.13), custom_call_target="tpu_custom_call" | custom-call | tf_op jit(solution)/shard_map/blocks/pallas_call | solution.py:483
  101.0 2.4 %copy.8 = bf16[1,384,1536]{2,1,0:T(8,128)(2,1)} copy(bf16[1,384,1536]{2,1,0:T(8,128)(2,1)} %bitcast.8) | data formatting | bytes 2359296

commit v4 on v3

--- a/solution.py
+++ b/solution.py
@@ -28,8 +28,8 @@
 
 def kernel(
     x_hbm, stale_hbm, proj_hbm, mod_hbm, pattern_ref, order_ref, out_ref,
-    w, dense, turned, stage, xb, st, hidden, q, kv, o, rs, sl, su, xl, xu, fr, marks, mod_ref,
-    loc_sem, zs, zr, xs, xr, d1s, d1r, d2s, d2r, rim_s, rim_r, str_s, str_r, out_sem,
+    w, dense, turned, xb, st, hidden, q, kv, o, rs, sl, su, xl, xu, fr, marks, mod_ref,
+    loc_sem, zs, zr, xs, xr, d1s, d1r, d2s, d2r, rim_s, rim_r, str_s, str_r,
 ):
     section = lax.axis_index("section")
     tile = lax.axis_index("tile")
@@ -235,6 +235,10 @@
             kv[0, g, m - 1] = low[0:TILE]
             fr[g, m - 1] = low[TILE:count]
 
+    def columns_of(g):
+        start = g * WIDE
+        return pl.ds(start if isinstance(g, int) else pl.multiple_of(start, WIDE), WIDE)
+
     def attend(g, turn, other, low, high, stream, ready):
         def window(k):
             return jnp.concatenate([kv[0, g, k], other(k), low(k), high(k)], axis=0)
@@ -243,7 +247,7 @@
         values = window(1)
         queries = q[g]
         mark = marks[turn]
-        gate = mod_ref[2:3, pl.ds(pl.multiple_of(g * WIDE, WIDE), WIDE)]
+        gate = mod_ref[2:3, columns_of(g)]
         for h in range(WIDE // HEAD):
             cols = slice(h * HEAD, (h + 1) * HEAD)
             scores = lax.dot_general(
@@ -256,17 +260,11 @@
             o[turn, g, :, cols] = (stream[:, cols] + gate[:, cols] * attended).astype(jnp.bfloat16)
             ready(g, h)
 
-    def out_copy(j, g):
-        rows = pl.ds(j * TILE, TILE)
-        cols = pl.ds(pl.multiple_of(g * WIDE, WIDE), WIDE)
-        return pltpu.make_async_copy(stage.at[j, g], out_ref.at[rows, cols], out_sem.at[j, g])
-
     def put_out(g):
         early, late = o[0, g], o[1, g]
-        stage[0, g] = pick(j0, late, early).astype(jnp.bfloat16)
-        stage[1, g] = pick(j0, early, late).astype(jnp.bfloat16)
-        for j in range(2):
-            out_copy(j, g).start()
+        cols = pl.ds(g * WIDE, WIDE)
+        out_ref[pl.ds(0, TILE), cols] = pick(j0, late, early).astype(jnp.bfloat16)
+        out_ref[pl.ds(TILE, TILE), cols] = pick(j0, early, late).astype(jnp.bfloat16)
 
     def lay_out(p):
         d1_copy(p).wait_recv()
@@ -421,7 +419,7 @@
     source = jnp.where(section == 0, 1, 0)
     modulate([lambda g=g: rs[source, g].astype(jnp.float32) for g in range(GROUPS)], 0, TILE)
 
-    def second_turn(g, carry):
+    def second_turn(g):
         project_again(g)
         attend(
             g, 1, lambda n: kv[1, g, n],
@@ -430,9 +428,9 @@
             rs[source, g].astype(jnp.float32), lambda g, h: None,
         )
         put_out(g)
-        return carry
-
-    lax.fori_loop(0, GROUPS, second_turn, 0)
+
+    for g in range(GROUPS):
+        second_turn(g)
 
     for cp in x_own() + rims:
         cp.wait_send()
@@ -441,9 +439,6 @@
             z_copy(part, way, z).wait_send()
     d1_copy(z).wait_send()
     d2_copy(z).wait_send()
-    for j in range(2):
-        for g in range(GROUPS):
-            out_copy(j, g).wait()
 
     for g, h in each_part:
         stream_copy(g, h).wait_send()
@@ -482,15 +477,14 @@
     bf16 = jnp.bfloat16
     out = pl.pallas_call(
         kernel,
-        out_shape=jax.ShapeDtypeStruct((2 * TILE, FEAT), bf16),
+        out_shape=pltpu.VMEM((2 * TILE, FEAT), bf16),
         in_specs=[pl.BlockSpec(memory_space=pl.ANY)] * 4
         + [pl.BlockSpec(memory_space=pltpu.VMEM)] * 2,
-        out_specs=pl.BlockSpec(memory_space=pl.ANY),
+        out_specs=pl.BlockSpec(memory_space=pltpu.VMEM),
         scratch_shapes=[
             vmem((PLANES, 4, 3, COLS, FEAT), bf16),
             vmem((GROUPS, 3, 4, 4 * COLS, FEAT), bf16),
             vmem((GROUPS, FEAT, 3 * WIDE), bf16),
-            vmem((2, GROUPS, TILE, WIDE), bf16),
             vmem((GROUPS, 2 * TILE, WIDE), bf16),
             vmem((GROUPS, 2, 2 * TILE, WIDE), bf16),
             vmem((TILE + RIM, FEAT), bf16),
@@ -518,7 +512,6 @@
             dma((4,)),
             dma((GROUPS, WIDE // HEAD)),
             dma((GROUPS, WIDE // HEAD)),
-            dma((2, GROUPS)),
         ],
         compiler_params=pltpu.CompilerParams(
             collective_id=0, has_side_effects=True, vmem_limit_bytes=58 * 2**20

time: 104 us -> 100 us (0.962)
  Pallas kernels: 101 us -> 99.3 us
  local copies, waits for them, and re-layouts: 2.36 us -> 1.02 us
    pallas_call x1, Pallas kernels: 101 us -> 99.3 us  [shards(): pl.pallas_call(kernel, out_shape=pltpu.VMEM((2 * TILE, FEAT), bf16), in_s...]
    unnamed x1, local copies, waits for them, and re-layouts: 2.36 us -> 1.02 us
where the time goes in v4:
time: 100 us
  Pallas kernels  99.3 us (99%)
  local copies, waits for them, and re-layouts  1.02 us (1%)
    pallas_call x1, Pallas kernels, shards(): pl.pallas_call(kernel, out_shape=pltpu.VMEM((2 * TILE, FEAT), bf16), in_s...  99.3 us

profile of v4, /device:TPU:1, one launch (start us, length us, event | category | flops | bytes accessed | tf_op | source)
XLA Modules:
  0.0 100.4 jit_solution(12304712424384301737)
XLA Ops:
  0.0 99.3 %blocks.1 = bf16[384,1536]{1,0:T(8,128)(2,1)S(1)} custom-call(bf16[384,1536]{1,0:T(8,128)(2,1)} %bitcast.10, bf16[384,3072]{1,0:T(8,128)(2,1)} %bitcast.9, bf16[3,24,1536]{2,1,0:T(8,128)(2,1)} %bitcast.11, f32[3,1,1536]{2,1,0:T(1,128)} %bitcast.12, s32[2,4]{1,0:T(2,128)} %pattern_ref.1, s32[1,2]{1,0:T(1,128)} %bitcast.13), custom_call_target="tpu_custom_call" | custom-call | tf_op jit(solution)/shard_map/blocks/pallas_call | solution.py:478
  99.4 1.0 %copy.8 = bf16[1,384,1536]{2,1,0:T(8,128)(2,1)} copy(bf16[1,384,1536]{2,1,0:T(8,128)(2,1)S(1)} %bitcast.8) | data formatting | bytes 2359296

commit v5 on v4

--- a/solution.py
+++ b/solution.py
@@ -19,7 +19,7 @@
 WIDE = FEAT // GROUPS
 HEAD = FEAT // HEADS
 WINDOW = 2 * TILE + 2 * RIM
-DUP = 768
+DUP = 1024
 EPS = 1e-06
 MESH = pl.DeviceIdType.MESH
 NT = (((1,), (1,)), ((), ()))

time: 100 us -> 101 us (1.010)
  no operation moved by 1% of the time
where the time goes in v5:
time: 101 us; the launch traced here: 100 us
  Pallas kernels  99.4 us (98%)
  local copies, waits for them, and re-layouts  1.02 us (1%)
    pallas_call x1, Pallas kernels, shards(): pl.pallas_call(kernel, out_shape=pltpu.VMEM((2 * TILE, FEAT), bf16), in_s...  99.4 us

profile of v5, /device:TPU:1, one launch (start us, length us, event | category | flops | bytes accessed | tf_op | source)
XLA Modules:
  0.0 100.4 jit_solution(11176780737940156493)
XLA Ops:
  0.0 99.4 %blocks.1 = bf16[384,1536]{1,0:T(8,128)(2,1)S(1)} custom-call(bf16[384,1536]{1,0:T(8,128)(2,1)} %bitcast.10, bf16[384,3072]{1,0:T(8,128)(2,1)} %bitcast.9, bf16[3,24,1536]{2,1,0:T(8,128)(2,1)} %bitcast.11, f32[3,1,1536]{2,1,0:T(1,128)} %bitcast.12, s32[2,4]{1,0:T(2,128)} %pattern_ref.1, s32[1,2]{1,0:T(1,128)} %bitcast.13), custom_call_target="tpu_custom_call" | custom-call | tf_op jit(solution)/shard_map/blocks/pallas_call | solution.py:478
  99.4 1.0 %copy.8 = bf16[1,384,1536]{2,1,0:T(8,128)(2,1)} copy(bf16[1,384,1536]{2,1,0:T(8,128)(2,1)S(1)} %bitcast.8) | data formatting | bytes 2359296
